TPU v7x, 256 devices: a whole 4x4x8 slice. The times are simulated.
256 devices in a mesh: dp: 16 (over y, x), tensor: 16 (over z, core).
Axes of the slice: x: 4, y: 4, z: 8, core: 2. Of those that a mesh axis runs over, the one named last changes fastest.
Arguments:
- head_out: bfloat16 [1024, 8192], P('dp', 'tensor'), may hold values from -9 to 9
- residual: bfloat16 [1024, 8192], P('tensor', 'dp'), may hold values from -9 to 9
- class_ids: int32 [1024], replicated, may hold values from 0 to 255
- head_mask: int32 [64], P('tensor'), may hold values 0 or 1
- out_weight: bfloat16 [8192, 8192], P('tensor', 'dp'), may hold values from -0.0625 to 0.0625
- norm_gain: bfloat16 [8192], P('dp'), may hold values from 0.5 to 1.5
- gate_up: bfloat16 [8192, 2, 14336], P('dp', None, 'tensor'), may hold values from -0.0625 to 0.0625
- down_weight: bfloat16 [14336, 8192], P('tensor', 'dp'), may hold values from -0.046875 to 0.046875
Outputs:
- layer_out: bfloat16 [1024, 8192], P('tensor', 'dp')
All inputs are finite; a program needn't handle non-finite values. No bound on the sum of `head_mask` on one device may be relied on, other than what follows from the above.
Results may differ from a plain program's by a relative error of at most 0.0066.
Values may be sent and summed in bfloat16 or wider, within the bound.
A program may use at most 64 MiB of HBM per device.

v0:
```python
import jax
import jax.numpy as jnp
from jax import lax
from jax.sharding import PartitionSpec as P

D = 8192
HEAD_DIM = 128
CLASSES = 256


norm_eps = 1e-05


def class_table(onehot, rows):
    totals = lax.dot_general(
        onehot, rows, (((0,), (0,)), ((), ())), preferred_element_type=jnp.float32
    )
    counts = jnp.sum(onehot.astype(jnp.float32), axis=0)
    return (totals, counts)


def local(head_out, residual, class_ids, head_mask, out_weight, norm_gain, gate_up, down_weight):
    classes = jnp.arange(CLASSES, dtype=jnp.int32)
    ablate = jnp.repeat(head_mask, HEAD_DIM) == 1
    gathered = lax.all_gather(head_out, "dp", axis=0, tiled=True)
    onehot = (class_ids[:, None] == classes[None, :]).astype(jnp.bfloat16)
    totals, counts = class_table(onehot, gathered)
    class_means = (totals / jnp.maximum(counts, 1.0)[:, None]).astype(jnp.bfloat16)
    looked = jnp.dot(onehot, class_means, preferred_element_type=jnp.float32).astype(jnp.bfloat16)
    rows_all = jnp.where(ablate[None, :], looked, gathered)
    row_block = rows_all
    attended = lax.psum_scatter(
        jnp.dot(row_block, out_weight, preferred_element_type=jnp.float32),
        "tensor",
        scatter_dimension=0,
        tiled=True,
    )
    stream = (residual.astype(jnp.float32) + attended).astype(jnp.bfloat16)
    stream_all = lax.all_gather(stream, "tensor", axis=0, tiled=True)
    stream_wide = stream_all.astype(jnp.float32)
    part_squares = jnp.sum(stream_wide * stream_wide, axis=1)
    scaled = (stream_wide * norm_gain.astype(jnp.float32)[None, :]).astype(jnp.bfloat16)
    ff_here = down_weight.shape[0]
    part_proj = jnp.dot(
        scaled, gate_up.reshape(gate_up.shape[0], 2 * ff_here), preferred_element_type=jnp.float32
    )
    projection, squares = lax.psum((part_proj, part_squares), "dp")
    inverse = lax.rsqrt(squares / D + norm_eps)
    gate_part = projection[:, :ff_here] * inverse[:, None]
    up_part = projection[:, ff_here:] * inverse[:, None]
    hidden_all = (jax.nn.silu(gate_part) * up_part).astype(jnp.bfloat16)
    row_block = hidden_all
    lowered = lax.psum_scatter(
        jnp.dot(row_block, down_weight, preferred_element_type=jnp.float32),
        "tensor",
        scatter_dimension=0,
        tiled=True,
    )
    return (stream.astype(jnp.float32) + lowered).astype(jnp.bfloat16)


def solution(mesh):
    in_specs = (
        P("dp", "tensor"),
        P("tensor", "dp"),
        P(),
        P("tensor"),
        P("tensor", "dp"),
        P("dp"),
        P("dp", None, "tensor"),
        P("tensor", "dp"),
    )
    out_specs = P("tensor", "dp")
    return jax.shard_map(local, mesh=mesh, in_specs=in_specs, out_specs=out_specs, check_vma=False)
```

profile of v0, /device:TPU:32, one launch (start us, length us, event | category | flops | bytes accessed | tf_op | source)
XLA Modules:
  0.0 381.4 jit_solution(1150167072119328582)
XLA Ops:
  6.5 0.0 copy-start
  6.5 0.7 all-gather.3.cloned.1.call-update
  7.3 0.0 reduce-scatter.3.cloned.1.call-start
  7.3 0.9 convert_reduce_fusion
  8.2 0.7 broadcast_compare_fusion
  8.9 0.1 broadcast_bitcast_fusion
  9.0 51.2 %all-gather.3.cloned.1.call-done = bf16[1024,512]{1,0:T(8,128)(2,1)} async-done(((bf16[64,512]{1,0:T(8,128)(2,1)}), bf16[1024,512]{1,0:T(8,128)(2,1)}) %all-gather.3.cloned.1.call-update) | async-done | bytes 1048592 | tf_op jit(solution)/shard_map/all_gather | solution.py:25
  60.2 2.0 fusion.8
  62.2 0.0 copy-start.4
  62.2 0.0 copy-start.5
  62.2 0.0 copy-start.1
  62.2 3.9 %fusion.7 = f32[1024,512]{1,0:T(8,128)} fusion(bf16[512,512]{1,0:T(8,128)(2,1)} %param.12, bf16[1024,512]{1,0:T(8,128)(2,1)} %all-gather.3.cloned.1.call-done, bf16[256,512]{1,0:T(8,128)(2,1)S(1)} %fusion.8, pred[512]{0:T(512)(128)(4,1)S(1)} %broadcast_bitcast_fusion, s32[1024]{0:T(1024)} %param.10), kind=kOutput, calls=%fused_computation.11 | convolution fusion | flops 806617088 | bytes 3936768 | tf_op jit(solution)/shard_map/dot_general | solution.py:33
  66.1 0.0 reduce-scatter.3.cloned.1.call-update
  66.2 0.0 all-gather.5.cloned.1.call-start
  66.2 55.5 %reduce-scatter.3.cloned.1.call-done = f32[64,512]{1,0:T(8,128)} async-done(((f32[1024,512]{1,0:T(8,128)}), f32[64,512]{1,0:T(8,128)}) %reduce-scatter.3.cloned.1.call-update) | async-done | bytes 131088 | tf_op jit(solution)/shard_map/reduce_scatter | solution.py:32
  121.7 1.6 add_convert_fusion.1
  123.3 0.0 all-gather.5.cloned.1.call-update
  123.3 0.0 all-reduce.2.cloned.1.call-start
  123.4 0.0 copy-done.5
  123.4 1.5 copy.9
  124.9 38.4 %all-gather.5.cloned.1.call-done = bf16[1024,512]{1,0:T(8,128)(2,1)} async-done(((bf16[64,512]{1,0:T(8,128)(2,1)}), bf16[1024,512]{1,0:T(8,128)(2,1)}) %all-gather.5.cloned.1.call-update) | async-done | bytes 1048592 | tf_op jit(solution)/shard_map/all_gather | solution.py:39
  163.3 6.9 %fusion.9 = f32[1024,1792]{1,0:T(8,128)} fusion(bf16[512,1792]{1,0:T(8,128)(2,1)} %bitcast.10, bf16[1024,512]{1,0:T(8,128)(2,1)} %all-gather.5.cloned.1.call-done, f32[512]{0:T(512)S(1)} %convert_element_type.44), kind=kOutput, calls=%fused_computation.14 | convolution fusion | flops 1880621056 | bytes 10225664 | tf_op jit(solution)/shard_map/dot_general | solution.py:44
  170.3 0.0 all-reduce.2.cloned.1.call-update
  170.3 0.0 reduce-scatter.5.cloned.1.call-start
  170.3 1.1 copy-done.2
  171.5 0.3 fusion.3
  171.8 41.6 %psum.15 = f32[1024]{0:T(1024)S(1)} all-reduce(f32[1024]{0:T(1024)S(1)} %fusion.3), channel_id=1, replica_groups=mesh['dp'=16,'tensor'=16] {'dp'}, use_global_device_ids=true, to_apply=%region_4.5 | all-reduce | flops 1024 | bytes 8192 | tf_op jit(solution)/shard_map/psum | solution.py:47
  213.4 98.1 %all-reduce.2.cloned.1.call-done = f32[1024,1792]{1,0:T(8,128)} async-done(((f32[1024,1792]{1,0:T(8,128)}), f32[1024,1792]{1,0:T(8,128)}) %all-reduce.2.cloned.1.call-update) | async-done | bytes 7340048 | tf_op jit(solution)/shard_map/psum | solution.py:47
  311.5 5.9 %fusion.4 = f32[1024,512]{1,0:T(8,128)} fusion(bf16[896,512]{1,0:T(8,128)(2,1)S(1)} %copy-done, f32[1024,1792]{1,0:T(8,128)} %all-reduce.2.cloned.1.call-done, f32[1024]{0:T(1024)S(1)} %add_rsqrt_fusion), kind=kOutput, calls=%fused_computation.8 | convolution fusion | flops 946864128 | bytes 10358784 | tf_op jit(solution)/shard_map/dot_general | solution.py:54
  317.4 0.0 reduce-scatter.5.cloned.1.call-update
  317.4 56.0 %reduce-scatter.5.cloned.1.call-done = f32[64,512]{1,0:T(8,128)} async-done(((f32[1024,512]{1,0:T(8,128)}), f32[64,512]{1,0:T(8,128)}) %reduce-scatter.5.cloned.1.call-update) | async-done | bytes 131088 | tf_op jit(solution)/shard_map/reduce_scatter | solution.py:53
  373.4 1.5 add_convert_fusion
  (10 shorter events, 0.0 us)
Async XLA Ops:
  6.5 304.9 %copy-start = (bf16[896,512]{1,0:T(8,128)(2,1)S(1)}, bf16[896,512]{1,0:T(8,128)(2,1)}, u32[]{:S(2)}) copy-start(bf16[896,512]{1,0:T(8,128)(2,1)} %param.15) | copy-start | bytes 2752516
  6.5 53.6 %all-gather.3.cloned.1.call-start = ((), (), s32[]{:S(2)}) async-start(), calls=%async_computation.2 | async-start | bytes 1114112 | tf_op jit(solution)/shard_map/all_gather | solution.py:25
  7.3 114.5 %reduce-scatter.3.cloned.1.call-start = ((), (), s32[]{:S(2)}) async-start(), calls=%async_computation.3 | async-start | bytes 2228224 | tf_op jit(solution)/shard_map/reduce_scatter | solution.py:32
  62.2 59.5 %copy-start.4 = (bf16[64,512]{1,0:T(8,128)(2,1)S(1)}, bf16[64,512]{1,0:T(8,128)(2,1)}, u32[]{:S(2)}) copy-start(bf16[64,512]{1,0:T(8,128)(2,1)} %param.9) | copy-start | bytes 196612
  62.2 61.2 %copy-start.5 = (bf16[512]{0:T(512)(128)(2,1)S(1)}, bf16[512]{0:T(512)(128)(2,1)}, u32[]{:S(2)}) copy-start(bf16[512]{0:T(512)(128)(2,1)} %param.13) | copy-start | bytes 3076
  62.2 61.2 %copy-start.1 = (bf16[512,2,896]{2,1,0:T(2,128)(2,1)S(1)}, bf16[512,2,896]{2,1,0:T(2,128)(2,1)}, u32[]{:S(2)}) copy-start(bf16[512,2,896]{2,1,0:T(2,128)(2,1)} %param.14) | copy-start | bytes 5505028
  66.2 97.2 %all-gather.5.cloned.1.call-start = ((), (), s32[]{:S(2)}) async-start(), calls=%async_computation.4 | async-start | bytes 1114112 | tf_op jit(solution)/shard_map/all_gather | solution.py:39
  123.3 188.1 %all-reduce.2.cloned.1.call-start = ((), (), s32[]{:S(2)}) async-start(), calls=%async_computation.5 | async-start | bytes 14680064 | tf_op jit(solution)/shard_map/psum | solution.py:47
  170.3 1.2 copy-start.2
  170.3 203.1 %reduce-scatter.5.cloned.1.call-start = ((), (), s32[]{:S(2)}) async-start(), calls=%async_computation.6 | async-start | bytes 2228224 | tf_op jit(solution)/shard_map/reduce_scatter | solution.py:53
  213.4 160.0 %copy-start.3 = (bf16[64,512]{1,0:T(8,128)(2,1)S(1)}, bf16[64,512]{1,0:T(8,128)(2,1)}, u32[]{:S(2)}) copy-start(bf16[64,512]{1,0:T(8,128)(2,1)} %add_convert_fusion.1) | copy-start | bytes 196612
Sparse Core Ops, SparseCore 0:
  9.8 50.3 all-gather.2
  66.3 55.4 reduce-scatter.2
  123.6 39.7 all-gather.4
  170.4 141.0 all-reduce.1
  317.5 55.7 reduce-scatter.4
where the time goes:
time: 385 us; the launch traced here: 381 us
  waiting for transfers between devices  300 us (78%)
  blocking collectives  41.6 us (11%)
  matrix products  18.8 us (5%)
  between operations  13.2 us (3%)
  other arithmetic  4.95 us (1%)
    psum x1, waiting for transfers between devices, local(): projection, squares = lax.psum((part_proj, part_squares), 'dp')  98.1 us
    reduce_scatter x1, waiting for transfers between devices, local(): lax.psum_scatter(jnp.dot(row_block, down_weight, preferred_element_type=j...  56 us
    reduce_scatter x1, waiting for transfers between devices, local(): lax.psum_scatter(jnp.dot(row_block, out_weight, preferred_element_type=jn...  55.5 us
    all_gather x1, waiting for transfers between devices, local(): gathered = lax.all_gather(head_out, 'dp', axis=0, tiled=True)  51.2 us
    psum x1, blocking collectives, local(): projection, squares = lax.psum((part_proj, part_squares), 'dp')  41.6 us
    all_gather x1, waiting for transfers between devices, local(): stream_all = lax.all_gather(stream, 'tensor', axis=0, tiled=True)  38.4 us
  transfers between devices with their start and end apart: 5, of which 5 were waited for; matrix products, arithmetic and copies ran while one was open for 1% of the time, Pallas kernels for 0%

commit v1 on v0

v1 whole, which is shorter than its diff:
```python
import functools

import jax
import jax.numpy as jnp
from jax import lax
from jax.experimental import pallas as pl
from jax.experimental.pallas import tpu as pltpu
from jax.sharding import PartitionSpec as P

MESH = pl.DeviceIdType.MESH
BF16 = jnp.bfloat16
F32 = jnp.float32
D = 8192
HEAD_DIM = 128
CLASSES = 256
EPS = 1e-05
TOKENS = 1024
W = 512
FF = 896
NQ = 2
R = 64 // NQ
ORDERS = ((3, 2, 1, 0), (2, 3, 0, 1), (1, 0, 3, 2), (0, 1, 2, 3))
D_WIDTH = (512, 512, 512, 384)
E_WIDTH = (256, 256, 256, 128)


def dot(a, b):
    return jnp.dot(a, b, preferred_element_type=F32)


def kernel(ho, res, ids, mask, ow, gain, gu, dw, out,
           ow_v, gu_v, dw_v, res_v, g, oh, oht, a, ar, az, st, p, r1, r2, r3, r4, h0, h1, h2, h3, f, fr, fz,
           load_sem, a_s, a_r, b_s, b_r, bz_s, bz_r, cz_s, cz_r, c_s, c_r, d_s, d_r, e_s, e_r, f_s, f_r, fz_s, fz_r):
    dp = lax.axis_index("dp")
    tn = lax.axis_index("tensor")
    y, x = dp // 4, dp % 4
    z, c = tn // 2, tn % 2
    rs = (r1, r2, r3, r4)
    hs = (h0, h1, h2, h3)
    bits = (y // 2, (y + y // 2) % 2, x // 2, (x + x // 2) % 2)
    near = (
        ((3 - y) * 4 + x, tn),
        ((y + 1 - 2 * (y % 2)) * 4 + x, tn),
        (y * 4 + 3 - x, tn),
        (y * 4 + x + 1 - 2 * (x % 2), tn),
    )
    sibling = (dp, z * 2 + 1 - c)

    def x_peer(k):
        return (y * 4 + (x + k) % 4, tn)

    def y_peer(k):
        return (((y + k) % 4) * 4 + x, tn)

    def z_peer(k):
        return (dp, ((z + k) % 8) * 2 + c)

    sends = []

    def send(src, dst, ssem, rsem, to):
        cp = pltpu.make_async_remote_copy(src_ref=src, dst_ref=dst, send_sem=ssem, recv_sem=rsem,
                                          device_id=to, device_id_type=MESH)
        cp.start()
        sends.append(cp)

    def arrived(ref, ssem, rsem):
        pltpu.make_async_remote_copy(src_ref=ref, dst_ref=ref, send_sem=ssem, recv_sem=rsem,
                                     device_id=sibling, device_id_type=MESH).wait_recv()

    loads = [
        pltpu.make_async_copy(ho.at[:, 0:256], g.at[0, y, x], load_sem.at[0]),
        pltpu.make_async_copy(ho.at[:, 256:512], g.at[1, y, x], load_sem.at[1]),
        pltpu.make_async_copy(ow, ow_v, load_sem.at[2]),
        pltpu.make_async_copy(gu, gu_v, load_sem.at[3]),
        pltpu.make_async_copy(dw, dw_v, load_sem.at[4]),
        pltpu.make_async_copy(res, res_v, load_sem.at[5]),
    ]
    for cp in loads:
        cp.start()

    barrier = pltpu.get_barrier_semaphore()
    peers = [x_peer(k) for k in (1, 2, 3)] + [y_peer(k) for k in (1, 2, 3)] + [z_peer(k) for k in range(1, 8)] + [sibling]
    for to in peers:
        pl.semaphore_signal(barrier, inc=1, device_id=to, device_id_type=MESH)
    pl.semaphore_wait(barrier, len(peers))

    loads[0].wait()
    loads[1].wait()
    for k in (1, 2, 3):
        send(g.at[0, y, x], g.at[0, y, x], a_s.at[0, k - 1], a_r.at[0, k - 1], x_peer(k))
        send(g.at[1, y, x], g.at[1, y, x], a_s.at[1, k - 1], a_r.at[1, k - 1], y_peer(k))
    ids_row = ids[...]
    same = lax.broadcasted_iota(jnp.int32, (CLASSES, TOKENS), 0) == ids_row
    onehot = same.astype(F32)
    counts = jnp.sum(onehot, axis=1, keepdims=True)
    oh[...] = onehot.astype(BF16)
    oht[...] = onehot.T.astype(BF16)
    for k in (1, 2, 3):
        arrived(g.at[0, y, x], a_s.at[0, k - 1], a_r.at[0, k - 1])
        arrived(g.at[1, y, x], a_s.at[1, k - 1], a_r.at[1, k - 1])
    for k in (1, 2, 3):
        send(g.at[0, y], g.at[0, y], a_s.at[2, k - 1], a_r.at[2, k - 1], y_peer(k))
        send(g.at[1, :, x], g.at[1, :, x], a_s.at[3, k - 1], a_r.at[3, k - 1], x_peer(k))
    for k in (1, 2, 3):
        arrived(g.at[0, y], a_s.at[2, k - 1], a_r.at[2, k - 1])
        arrived(g.at[1, :, x], a_s.at[3, k - 1], a_r.at[3, k - 1])

    means = []
    for h in (0, 1):
        totals = dot(oh[...], g[h].reshape(TOKENS, 256))
        means.append((totals / jnp.maximum(counts, 1.0)).astype(BF16))
    lane_head = lax.broadcasted_iota(jnp.int32, (1, 256), 1) // HEAD_DIM
    ablate = [jnp.where(lane_head == 0, mask[2 * h], mask[2 * h + 1]) == 1 for h in (0, 1)]
    loads[2].wait()
    for i in range(4):
        rows = oht[256 * i:256 * i + 256]
        total = None
        for h in (0, 1):
            looked = dot(rows, means[h])
            patched = jnp.where(ablate[h], looked, g[h, i].reshape(256, 256).astype(F32)).astype(BF16)
            part = dot(patched, ow_v[256 * h:256 * h + 256])
            total = part if total is None else total + part
        a[2 * i:2 * i + 2] = total.astype(BF16).reshape(2, 2, 64, W)

    def rows_of(q):
        return pl.ds(R * q, R)

    def pair_send(q, buf, recv, ssem, rsem):
        send(buf.at[:, 1 - c, rows_of(q)], recv.at[q], ssem.at[q], rsem.at[q], sibling)

    def ring_send(q, buf, recv, ssem, rsem, zrecv, zs, zr):
        arrived(recv.at[q], ssem.at[q], rsem.at[q])
        both = buf[:, c, rows_of(q)].astype(F32) + recv[q].astype(F32)
        buf[:, c, rows_of(q)] = both.astype(BF16)
        for k in (4, 3, 5, 2, 6, 1, 7):
            send(buf.at[(z + k) % 8, c, rows_of(q)], zrecv.at[q, k], zs.at[q, k], zr.at[q, k], z_peer(k))

    def ring_total(q, buf, zrecv, zs, zr):
        total = buf[z, c, rows_of(q)].astype(F32)
        for k in (1, 7, 2, 6, 3, 5, 4):
            arrived(zrecv.at[q, k], zs.at[q, k], zr.at[q, k])
            total = total + zrecv[q, k].astype(F32)
        return total

    def b1(q):
        pair_send(q, a, ar, b_s, b_r)

    def b2(q):
        ring_send(q, a, ar, b_s, b_r, az, bz_s, bz_r)

    def c1(q):
        if q == 0:
            loads[5].wait()
        stream = res_v[rows_of(q)].astype(F32) + ring_total(q, a, az, bz_s, bz_r)
        st[z, c, rows_of(q)] = stream.astype(BF16)
        mine = st.at[z, c, rows_of(q)]
        for k in (4, 3, 5, 2, 6, 1, 7):
            send(mine, mine, cz_s.at[q, k], cz_r.at[q, k], z_peer(k))

    def c2(q):
        mine = st.at[z, c, rows_of(q)]
        for k in (1, 7, 2, 6, 3, 5, 4):
            arrived(mine, cz_s.at[q, k], cz_r.at[q, k])
        col = st.at[:, c, rows_of(q)]
        send(col, col, c_s.at[q], c_r.at[q], sibling)

    def cube(i, order, step, flip):
        at = [slice(None)] * 4
        for n in range(step):
            at[order[n]] = bits[order[n]]
        if flip:
            at[order[step]] = 1 - bits[order[step]]
        return tuple(at)

    def d_send(q, i, step):
        order = ORDERS[i]
        at = cube(i, order, step, True)
        if step > 0:
            total = p[(q, i) + at].astype(F32)
            for n in range(step):
                total = total + rs[n][(q, i) + at].astype(F32)
            p[(q, i) + at] = total.astype(BF16)
        lanes = (slice(None),) + (pl.ds(0, D_WIDTH[i]),)
        where = (q, i) + at + lanes
        send(p.at[where], rs[step].at[where], d_s.at[q, i, step], d_r.at[q, i, step], near[order[step]])

    def d_arrived(q, i, step):
        order = ORDERS[i]
        at = list(cube(i, order, step, False))
        at[order[step]] = bits[order[step]]
        lanes = (slice(None),) + (pl.ds(0, D_WIDTH[i]),)
        arrived(rs[step].at[(q, i) + tuple(at) + lanes], d_s.at[q, i, step], d_r.at[q, i, step])

    def d1(q):
        if q == 0:
            loads[3].wait()
        col = st.at[:, 1 - c, rows_of(q)]
        arrived(col, c_s.at[q], c_r.at[q])
        wide = st[:, :, rows_of(q)].reshape(16 * R, W).astype(F32)
        squares = jnp.sum(wide * wide, axis=1, keepdims=True)
        scaled = (wide * gain[...].astype(F32)).astype(BF16)
        for i in range(4):
            width = 512 if i < 3 else 256
            part = dot(scaled, gu_v[:, 512 * i:512 * i + width]).astype(BF16)
            p[q, i, :, :, :, :, :, 0:width] = part.reshape(2, 2, 2, 2, R, width)
            if i == 3:
                wide_squares = jnp.broadcast_to(squares, (16 * R, 128)).astype(BF16)
                p[q, i, :, :, :, :, :, 256:384] = wide_squares.reshape(2, 2, 2, 2, R, 128)
            d_send(q, i, 0)

    def d_next(q, step):
        for i in range(4):
            d_arrived(q, i, step - 1)
            d_send(q, i, step)

    def e_ref(q, i, step):
        order = ORDERS[i]
        at = [slice(None)] * 4
        for n in range(4 - step):
            at[order[n]] = bits[order[n]]
        return tuple(at)

    def e_send(q, i, step):
        where = (q,) + e_ref(q, i, step)
        dim = ORDERS[i][3 - step]
        send(hs[i].at[where], hs[i].at[where], e_s.at[q, i, step], e_r.at[q, i, step], near[dim])

    def e_arrived(q, i, step):
        at = list(e_ref(q, i, step))
        dim = ORDERS[i][3 - step]
        at[dim] = 1 - bits[dim]
        arrived(hs[i].at[(q,) + tuple(at)], e_s.at[q, i, step], e_r.at[q, i, step])

    def d5(q):
        sums = []
        for i in range(4):
            d_arrived(q, i, 3)
            at = (q, i) + tuple(bits)
            total = p[at].astype(F32)
            for n in range(4):
                total = total + rs[n][at].astype(F32)
            sums.append(total)
        inverse = lax.rsqrt(sums[3][:, 256:384] / D + EPS)

        def tile(n):
            return sums[n // 4][:, 128 * (n % 4):128 * (n % 4) + 128] * inverse

        for i in range(4):
            for n in range(E_WIDTH[i] // 128):
                gate, up = tile(2 * i + n), tile(7 + 2 * i + n)
                hidden = gate / (1.0 + jnp.exp(-gate)) * up
                hs[i][(q,) + tuple(bits) + (slice(None), slice(128 * n, 128 * n + 128))] = hidden.astype(BF16)
            e_send(q, i, 0)

    def e_next(q, step):
        for i in range(4):
            e_arrived(q, i, step - 1)
            e_send(q, i, step)

    def f1(q):
        if q == 0:
            loads[4].wait()
        total = None
        for i in range(4):
            e_arrived(q, i, 3)
            part = dot(hs[i][q].reshape(16 * R, E_WIDTH[i]), dw_v[256 * i:256 * i + E_WIDTH[i]])
            total = part if total is None else total + part
        f[:, :, rows_of(q)] = total.astype(BF16).reshape(8, 2, R, W)
        pair_send(q, f, fr, f_s, f_r)

    def f2(q):
        ring_send(q, f, fr, f_s, f_r, fz, fz_s, fz_r)

    def f3(q):
        total = st[z, c, rows_of(q)].astype(F32) + ring_total(q, f, fz, fz_s, fz_r)
        out[rows_of(q)] = total.astype(BF16)

    stages = [b1, b2, c1, c2, d1]
    stages += [functools.partial(d_next, step=s) for s in (1, 2, 3)] + [d5]
    stages += [functools.partial(e_next, step=s) for s in (1, 2, 3)] + [f1, f2, f3]
    for stage in stages:
        for q in range(NQ):
            stage(q)
    for cp in sends:
        cp.wait_send()


def local(head_out, residual, class_ids, head_mask, out_weight, norm_gain, gate_up, down_weight):
    hbm = pl.BlockSpec(memory_space=pl.ANY)
    vmem = pl.BlockSpec(memory_space=pltpu.VMEM)
    smem = pl.BlockSpec(memory_space=pltpu.SMEM)
    dma = pltpu.SemaphoreType.DMA
    cube = (NQ, 4, 2, 2, 2, 2, R, 512)
    return pl.pallas_call(
        kernel,
        out_shape=jax.ShapeDtypeStruct((64, W), BF16),
        in_specs=[hbm, hbm, vmem, smem, hbm, vmem, hbm, hbm],
        out_specs=vmem,
        scratch_shapes=[
            pltpu.VMEM((W, W), BF16),
            pltpu.VMEM((W, 2 * FF), BF16),
            pltpu.VMEM((FF, W), BF16),
            pltpu.VMEM((64, W), BF16),
            pltpu.VMEM((2, 4, 4, 64, 256), BF16),
            pltpu.VMEM((CLASSES, TOKENS), BF16),
            pltpu.VMEM((TOKENS, CLASSES), BF16),
            pltpu.VMEM((8, 2, 64, W), BF16),
            pltpu.VMEM((NQ, 8, R, W), BF16),
            pltpu.VMEM((NQ, 8, R, W), BF16),
            pltpu.VMEM((8, 2, 64, W), BF16),
            pltpu.VMEM(cube, BF16), pltpu.VMEM(cube, BF16), pltpu.VMEM(cube, BF16),
            pltpu.VMEM(cube, BF16), pltpu.VMEM(cube, BF16),
            *[pltpu.VMEM((NQ, 2, 2, 2, 2, R, w), BF16) for w in E_WIDTH],
            pltpu.VMEM((8, 2, 64, W), BF16),
            pltpu.VMEM((NQ, 8, R, W), BF16),
            pltpu.VMEM((NQ, 8, R, W), BF16),
            dma((6,)),
            dma((4, 3)), dma((4, 3)),
            dma((NQ,)), dma((NQ,)),
            dma((NQ, 8)), dma((NQ, 8)),
            dma((NQ, 8)), dma((NQ, 8)),
            dma((NQ,)), dma((NQ,)),
            dma((NQ, 4, 4)), dma((NQ, 4, 4)),
            dma((NQ, 4, 4)), dma((NQ, 4, 4)),
            dma((NQ,)), dma((NQ,)),
            dma((NQ, 8)), dma((NQ, 8)),
        ],
        compiler_params=pltpu.CompilerParams(
            collective_id=0, has_side_effects=True, vmem_limit_bytes=56 << 20
        ),
        name="layer",
    )(head_out, residual, class_ids.reshape(1, TOKENS), head_mask, out_weight, norm_gain.reshape(1, W),
      gate_up.reshape(W, 2 * FF), down_weight)


def solution(mesh):
    in_specs = (
        P("dp", "tensor"),
        P("tensor", "dp"),
        P(),
        P("tensor"),
        P("tensor", "dp"),
        P("dp"),
        P("dp", None, "tensor"),
        P("tensor", "dp"),
    )
    return jax.shard_map(local, mesh=mesh, in_specs=in_specs, out_specs=P("tensor", "dp"), check_vma=False)
```

time: 385 us -> 116 us (0.30)
  waiting for transfers between devices: 300 us -> 0 us
  Pallas kernels: 0 us -> 108 us
  blocking collectives: 41.6 us -> 0 us
  matrix products: 18.8 us -> 0 us
  between operations: 13.2 us -> 0.01 us
  other arithmetic: 4.95 us -> 0 us
    reduce_scatter x2 -> x0, waiting for transfers between devices: 111 us -> none  [the longest x1 56 us: local(): lax.psum_scatter(jnp.dot(row_block, down_weight, preferred_element_type=j...]
    pallas_call x0 -> x1, Pallas kernels: none -> 108 us  [local(): pl.pallas_call(kernel, out_shape=jax.ShapeDtypeStruct((64, W), BF16), in_...]
    psum x1 -> x0, waiting for transfers between devices: 98.1 us -> none  [local(): projection, squares = lax.psum((part_proj, part_squares), 'dp')]
    all_gather x2 -> x0, waiting for transfers between devices: 89.6 us -> none  [the longest x1 51.2 us: local(): gathered = lax.all_gather(head_out, 'dp', axis=0, tiled=True)]
    psum x1 -> x0, blocking collectives: 41.6 us -> none  [local(): projection, squares = lax.psum((part_proj, part_squares), 'dp')]
    dot_general x4 -> x0, matrix products: 18.8 us -> none  [the longest x1 6.91 us: local(): jnp.dot(scaled, gate_up.reshape(gate_up.shape[0], 2 * ff_here), preferred...]
  transfers between devices with their start and end apart: 5 -> 0, of which waited for: 5 -> 0; matrix products, arithmetic and copies ran while one was open for 1% -> 0% of each run, Pallas kernels for 0% -> 0%
where the time goes in v1:
time: 116 us; the launch traced here: 114 us
  Pallas kernels  108 us (93%)
  local copies, waits for them, and re-layouts  5.76 us (5%)
    pallas_call x1, Pallas kernels, local(): pl.pallas_call(kernel, out_shape=jax.ShapeDtypeStruct((64, W), BF16), in_...  108 us
    unnamed x2, local copies, waits for them, and re-layouts  4.5 us

profile of v1, /device:TPU:32, one launch (start us, length us, event | category | flops | bytes accessed | tf_op | source)
XLA Modules:
  0.0 114.3 jit_solution(1041443619253833211)
XLA Ops:
  0.0 1.3 %reshape.10.gain = bf16[1,512]{1,0:T(2,128)(2,1)} reshape(bf16[512]{0:T(512)(128)(2,1)} %param.13) | data formatting | bytes 2048 | tf_op jit(solution)/shard_map/reshape | solution.py:332
  1.3 3.0 %copy.9 = bf16[64,8,2,896]{3,1,2,0:T(8,128)(2,1)} copy(bf16[64,8,2,896]{3,2,1,0:T(2,128)(2,1)} %bitcast.4) | data formatting | bytes 3670016
  4.3 108.5 %layer.1 = bf16[64,512]{1,0:T(8,128)(2,1)} custom-call(bf16[64,512]{1,0:T(8,128)(2,1)} %ho.1, bf16[64,512]{1,0:T(8,128)(2,1)} %res.1, s32[1,1024]{1,0:T(1,128)} %bitcast.5, s32[4]{0:T(128)} %mask.1, bf16[512,512]{1,0:T(8,128)(2,1)} %ow.1, bf16[1,512]{1,0:T(2,128)(2,1)} %reshape.10.gain, bf16[512,1792]{1,0:T(8,128)(2,1)} %bitcast.3, bf16[896,512]{1,0:T(8,128)(2,1)} %dw.1), custom_call_target="tpu_custom_call" | custom-call | tf_op jit(solution)/shard_map/layer/pallas_call | solution.py:294
  112.8 1.5 %copy.11 = bf16[64,512]{1,0:T(8,128)(2,1)} copy(bf16[64,512]{1,0:T(8,128)(2,1)} %layer.1) | data formatting | bytes 131072

commit v2 on v1

v2 whole, which is shorter than its diff:
```python
import functools

import jax
import jax.numpy as jnp
from jax import lax
from jax.experimental import pallas as pl
from jax.experimental.pallas import tpu as pltpu
from jax.sharding import PartitionSpec as P

MESH = pl.DeviceIdType.MESH
BF16 = jnp.bfloat16
F32 = jnp.float32
D = 8192
HEAD_DIM = 128
CLASSES = 256
EPS = 1e-05
TOKENS = 1024
W = 512
FF = 896
NQ = 2
R = 64 // NQ
RD = R // 2
ORDERS = ((3, 2, 1, 0), (2, 3, 0, 1), (1, 0, 3, 2), (0, 1, 2, 3))
E_TILES = ((0, 4), (4, 8), (8, 11), (11, 14))


def dot(a, b):
    return jnp.dot(a, b, preferred_element_type=F32)


def kernel(ho, res, ids, mask, ow, gain, gu, dw, out,
           ow_v, gu_in, gu_v, dw_v, res_v, g, oh, oht, a, ar, az, azh, ah, st, p, r1, r2, r3, r4, h0, h1, h2, h3, f, fz, fzh,
           load_sem, w_s, w_r, x_s, x_r, a_s, a_r, b_s, b_r, bz_s, bz_r, cz_s, cz_r, d_s, d_r, e_s, e_r, fz_s, fz_r):
    dp = lax.axis_index("dp")
    tn = lax.axis_index("tensor")
    y, x = dp // 4, dp % 4
    z, c = tn // 2, tn % 2
    rs = (r1, r2, r3, r4)
    hs = (h0, h1, h2, h3)
    bits = (y // 2, (y + y // 2) % 2, x // 2, (x + x // 2) % 2)
    near = (
        ((3 - y) * 4 + x, tn),
        ((y + 1 - 2 * (y % 2)) * 4 + x, tn),
        (y * 4 + 3 - x, tn),
        (y * 4 + x + 1 - 2 * (x % 2), tn),
    )
    sibling = (dp, z * 2 + 1 - c)

    def x_peer(k):
        return (y * 4 + (x + k) % 4, tn)

    def y_peer(k):
        return (((y + k) % 4) * 4 + x, tn)

    def z_peer(k):
        return (dp, ((z + k + 8) % 8) * 2 + c)

    def block(k):
        return (z + k + 8) % 8

    sends = []

    def send(src, dst, ssem, rsem, to):
        cp = pltpu.make_async_remote_copy(src_ref=src, dst_ref=dst, send_sem=ssem, recv_sem=rsem,
                                          device_id=to, device_id_type=MESH)
        cp.start()
        sends.append(cp)

    def arrived(ref, ssem, rsem):
        pltpu.make_async_remote_copy(src_ref=ref, dst_ref=ref, send_sem=ssem, recv_sem=rsem,
                                     device_id=sibling, device_id_type=MESH).wait_recv()

    loads = [
        pltpu.make_async_copy(ho.at[:, 0:256], g.at[0, y, x], load_sem.at[0]),
        pltpu.make_async_copy(ho.at[:, 256:512], g.at[1, y, x], load_sem.at[1]),
        pltpu.make_async_copy(gu, gu_in, load_sem.at[2]),
        pltpu.make_async_copy(dw, dw_v.at[0], load_sem.at[3]),
        pltpu.make_async_copy(ow, ow_v, load_sem.at[4]),
        pltpu.make_async_copy(res, res_v, load_sem.at[5]),
    ]
    for cp in loads:
        cp.start()

    barrier = pltpu.get_barrier_semaphore()
    peers = [x_peer(k) for k in (1, 2, 3)] + [y_peer(k) for k in (1, 2, 3)] + [z_peer(k) for k in (1, -1, 2, -2)] + [sibling]
    for to in peers:
        pl.semaphore_signal(barrier, inc=1, device_id=to, device_id_type=MESH)

    loads[2].wait()
    gu_v[0] = gu_in[:, 0, :]
    gu_v[1] = gu_in[:, 1, :]
    same = lax.broadcasted_iota(jnp.int32, (CLASSES, TOKENS), 0) == ids[...]
    onehot = same.astype(F32)
    counts = jnp.sum(onehot, axis=1, keepdims=True)
    oh[...] = onehot.astype(BF16)
    oht[...] = onehot.T.astype(BF16)
    loads[0].wait()
    loads[1].wait()
    loads[3].wait()
    pl.semaphore_wait(barrier, len(peers))

    first = ((x_peer, y_peer), (y_peer, x_peer))
    for k in (1, 3, 2):
        for h in (0, 1):
            send(g.at[h, y, x], g.at[h, y, x], x_s.at[h, k], x_r.at[h, k], first[h][0](k))
    for k in (1, 3, 2):
        for h in (0, 1):
            send(g.at[h, y, x], g.at[h, y, x], a_s.at[h, 0, k], a_r.at[h, 0, k], first[h][1](k))
    send(gu_v.at[0:2], gu_v.at[2:4], w_s.at[0], w_r.at[0], sibling)
    send(dw_v.at[0], dw_v.at[1], w_s.at[1], w_r.at[1], sibling)
    for j in (1, 3, 2):
        for h in (0, 1):
            got = g.at[h, y, (x - j + 4) % 4] if h == 0 else g.at[h, (y - j + 4) % 4, x]
            arrived(got, x_s.at[h, j], x_r.at[h, j])
            for k in (1, 3, 2):
                send(got, got, a_s.at[h, j, k], a_r.at[h, j, k], first[h][1](k))
    for j in range(4):
        for k in (1, 2, 3):
            for h in (0, 1):
                arrived(g.at[h, y, x], a_s.at[h, j, k], a_r.at[h, j, k])

    means = []
    for h in (0, 1):
        totals = dot(oh[...], g[h].reshape(TOKENS, 256))
        means.append((totals / jnp.maximum(counts, 1.0)).astype(BF16))
    lane_head = lax.broadcasted_iota(jnp.int32, (1, 256), 1) // HEAD_DIM
    ablate = [jnp.where(lane_head == 0, mask[2 * h], mask[2 * h + 1]) == 1 for h in (0, 1)]
    loads[4].wait()
    for i in range(4):
        rows = oht[256 * i:256 * i + 256]
        total = None
        for h in (0, 1):
            looked = dot(rows, means[h])
            patched = jnp.where(ablate[h], looked, g[h, i].reshape(256, 256).astype(F32)).astype(BF16)
            part = dot(patched, ow_v[256 * h:256 * h + 256])
            total = part if total is None else total + part
        a[2 * i:2 * i + 2] = total.astype(BF16).reshape(2, 2, 64, W)

    def rows_of(q):
        return pl.ds(R * q, R)

    def z_first(q, buf, recv, half, ss, sr):
        r = rows_of(q)
        low, high = pl.ds(R * q, R // 2), pl.ds(R * q + R // 2, R // 2)
        send(buf.at[block(3), r], recv.at[q, 2], ss.at[q, 2], sr.at[q, 2], z_peer(1))
        send(buf.at[block(-3), r], recv.at[q, 3], ss.at[q, 3], sr.at[q, 3], z_peer(-1))
        send(buf.at[block(4), low], half.at[q, 0], ss.at[q, 6], sr.at[q, 6], z_peer(2))
        send(buf.at[block(4), high], half.at[q, 1], ss.at[q, 7], sr.at[q, 7], z_peer(-2))
        send(buf.at[block(1), r], recv.at[q, 0], ss.at[q, 0], sr.at[q, 0], z_peer(1))
        send(buf.at[block(-1), r], recv.at[q, 1], ss.at[q, 1], sr.at[q, 1], z_peer(-1))

    def z_second(q, buf, recv, half, ss, sr):
        r = rows_of(q)
        for n, way in ((0, 2), (1, -2)):
            arrived(recv.at[q, 2 + n], ss.at[q, 2 + n], sr.at[q, 2 + n])
            arrived(half.at[q, n], ss.at[q, 6 + n], sr.at[q, 6 + n])
            total = buf[block(way), r].astype(F32) + recv[q, 2 + n].astype(F32)
            extra = half[q, n].astype(F32)
            zeros = jnp.zeros_like(extra)
            total = total + jnp.concatenate([extra, zeros] if n == 0 else [zeros, extra], axis=0)
            buf[block(way), r] = total.astype(BF16)
            send(buf.at[block(way), r], recv.at[q, 4 + n], ss.at[q, 4 + n], sr.at[q, 4 + n], z_peer(way))

    def z_total(q, own, recv, ss, sr):
        total = own
        for n in (0, 1, 4, 5):
            arrived(recv.at[q, n], ss.at[q, n], sr.at[q, n])
            total = total + recv[q, n].astype(F32)
        return total

    def b1(q):
        send(a.at[:, 1 - c, rows_of(q)], ar.at[q], b_s.at[q], b_r.at[q], sibling)

    def b2(q):
        arrived(ar.at[q], b_s.at[q], b_r.at[q])
        both = a[:, c, rows_of(q)].astype(F32) + ar[q].astype(F32)
        ah[:, rows_of(q)] = both.astype(BF16)
        z_first(q, ah, az, azh, bz_s, bz_r)

    def b3(q):
        z_second(q, ah, az, azh, bz_s, bz_r)

    def c1(q):
        if q == 0:
            loads[5].wait()
        r = rows_of(q)
        own = a[z, c, r].astype(F32) + ar[q, z].astype(F32)
        stream = res_v[r].astype(F32) + z_total(q, own, az, bz_s, bz_r)
        st[z, r] = stream.astype(BF16)
        mine = st.at[z, r]
        for n, way in ((2, 2), (3, -2), (0, 1), (1, -1)):
            send(mine, mine, cz_s.at[q, n], cz_r.at[q, n], z_peer(way))

    def c2(q):
        r = rows_of(q)
        low, high = pl.ds(R * q, R // 2), pl.ds(R * q + R // 2, R // 2)
        mine = st.at[z, r]
        for n, way, part in ((0, 1, low), (1, -1, high)):
            arrived(mine, cz_s.at[q, 2 + n], cz_r.at[q, 2 + n])
            far = block(-2 * way)
            send(st.at[far, r], st.at[far, r], cz_s.at[q, 4 + n], cz_r.at[q, 4 + n], z_peer(way))
            send(st.at[far, part], st.at[far, part], cz_s.at[q, 6 + n], cz_r.at[q, 6 + n], z_peer(2 * way))

    def cube(order, step, flip):
        at = [slice(None)] * 4
        for n in range(step):
            at[order[n]] = bits[order[n]]
        at[order[step]] = 1 - bits[order[step]] if flip else bits[order[step]]
        return tuple(at)

    def d_lanes(q, i):
        return (slice(None), pl.ds(0, FF + 128 if i == q else FF))

    def d_send(q, i, step):
        order = ORDERS[i]
        where = (q, i) + cube(order, step, True) + d_lanes(q, i)
        if step > 0:
            total = p[where].astype(F32)
            for n in range(step):
                total = total + rs[n][where].astype(F32)
            p[where] = total.astype(BF16)
        send(p.at[where], rs[step].at[where], d_s.at[q, i, step], d_r.at[q, i, step], near[order[step]])

    def d_arrived(q, i, step):
        where = (q, i) + cube(ORDERS[i], step, False) + d_lanes(q, i)
        arrived(rs[step].at[where], d_s.at[q, i, step], d_r.at[q, i, step])

    def d1(q):
        if q == 0:
            arrived(gu_v.at[0:2], w_s.at[0], w_r.at[0])
        r = rows_of(q)
        mine = st.at[z, r]
        for n in (0, 1, 4, 5):
            arrived(mine, cz_s.at[q, n], cz_r.at[q, n])
        for n in (6, 7):
            arrived(st.at[z, pl.ds(R * q, R // 2)], cz_s.at[q, n], cz_r.at[q, n])
        wide = st[:, r].reshape(8 * R, W).astype(F32)
        scaled = (wide * gain[...].astype(F32).reshape(1, W)).astype(BF16)
        for i in range(4):
            part = dot(scaled, gu_v[i]).astype(BF16)
            p[q, i, :, :, :, :, :, 0:FF] = part.reshape(2, 2, 2, 2, RD, FF)
            if i == q:
                squares = jnp.sum(wide * wide, axis=1, keepdims=True)
                squares = jnp.broadcast_to(squares, (8 * R, 128)).astype(BF16)
                p[q, i, :, :, :, :, :, FF:FF + 128] = squares.reshape(2, 2, 2, 2, RD, 128)
            d_send(q, i, 0)

    def d_next(q, step):
        for i in range(4):
            d_arrived(q, i, step - 1)
            d_send(q, i, step)

    def e_ref(q, i, step):
        order = ORDERS[i]
        at = [slice(None)] * 4
        for n in range(4 - step):
            at[order[n]] = bits[order[n]]
        return tuple(at)

    def e_send(q, i, step):
        where = (q,) + e_ref(q, i, step)
        dim = ORDERS[i][3 - step]
        send(hs[i].at[where], hs[i].at[where], e_s.at[q, i, step], e_r.at[q, i, step], near[dim])

    def e_arrived(q, i, step):
        at = list(e_ref(q, i, step))
        dim = ORDERS[i][3 - step]
        at[dim] = 1 - bits[dim]
        arrived(hs[i].at[(q,) + tuple(at)], e_s.at[q, i, step], e_r.at[q, i, step])

    def d5(q):
        sums = []
        for i in range(4):
            d_arrived(q, i, 3)
            at = (q, i) + tuple(bits) + d_lanes(q, i)
            total = p[at].astype(F32)
            for n in range(4):
                total = total + rs[n][at].astype(F32)
            sums.append(total)
        inverse = lax.rsqrt(sums[q][:, FF:FF + 128] / D + EPS)
        for i in range(4):
            for n in range(*E_TILES[i]):
                lanes = slice(128 * (n % 7), 128 * (n % 7) + 128)
                gate = sums[2 * (n // 7)][:, lanes] * inverse
                up = sums[2 * (n // 7) + 1][:, lanes] * inverse
                hidden = gate / (1.0 + jnp.exp(-gate)) * up
                at = 128 * (n - E_TILES[i][0])
                hs[i][(q,) + tuple(bits) + (slice(None), slice(at, at + 128))] = hidden.astype(BF16)
            e_send(q, i, 0)

    def e_next(q, step):
        for i in range(4):
            e_arrived(q, i, step - 1)
            e_send(q, i, step)

    def f1(q):
        if q == 0:
            arrived(dw_v.at[1], w_s.at[1], w_r.at[1])
        down = dw_v[...].reshape(2 * FF, W)
        total = None
        for i in range(4):
            e_arrived(q, i, 3)
            lo, hi = E_TILES[i]
            part = dot(hs[i][q].reshape(8 * R, 128 * (hi - lo)), down[128 * lo:128 * hi])
            total = part if total is None else total + part
        f[:, rows_of(q)] = total.astype(BF16).reshape(8, R, W)
        z_first(q, f, fz, fzh, fz_s, fz_r)

    def f2(q):
        z_second(q, f, fz, fzh, fz_s, fz_r)

    def f3(q):
        r = rows_of(q)
        total = z_total(q, f[z, r].astype(F32), fz, fz_s, fz_r)
        out[r] = (st[z, r].astype(F32) + total).astype(BF16)

    stages = [b1, b2, b3, c1, c2, d1]
    stages += [functools.partial(d_next, step=s) for s in (1, 2, 3)] + [d5]
    stages += [functools.partial(e_next, step=s) for s in (1, 2, 3)] + [f1, f2, f3]
    for stage in stages:
        for q in range(NQ):
            stage(q)
    for cp in sends:
        cp.wait_send()


def local(head_out, residual, class_ids, head_mask, out_weight, norm_gain, gate_up, down_weight):
    hbm = pl.BlockSpec(memory_space=pl.ANY)
    vmem = pl.BlockSpec(memory_space=pltpu.VMEM)
    smem = pl.BlockSpec(memory_space=pltpu.SMEM)
    dma = pltpu.SemaphoreType.DMA
    cube = (NQ, 4, 2, 2, 2, 2, RD, FF + 128)
    return pl.pallas_call(
        kernel,
        out_shape=jax.ShapeDtypeStruct((64, W), BF16),
        in_specs=[hbm, hbm, vmem, smem, hbm, vmem, hbm, hbm],
        out_specs=vmem,
        scratch_shapes=[
            pltpu.VMEM((W, W), BF16),
            pltpu.VMEM((W, 2, FF), BF16),
            pltpu.VMEM((4, W, FF), BF16),
            pltpu.VMEM((2, FF, W), BF16),
            pltpu.VMEM((64, W), BF16),
            pltpu.VMEM((2, 4, 4, 64, 256), BF16),
            pltpu.VMEM((CLASSES, TOKENS), BF16),
            pltpu.VMEM((TOKENS, CLASSES), BF16),
            pltpu.VMEM((8, 2, 64, W), BF16),
            pltpu.VMEM((NQ, 8, R, W), BF16),
            pltpu.VMEM((NQ, 6, R, W), BF16),
            pltpu.VMEM((NQ, 2, R // 2, W), BF16),
            pltpu.VMEM((8, 64, W), BF16),
            pltpu.VMEM((8, 64, W), BF16),
            *[pltpu.VMEM(cube, BF16) for _ in range(5)],
            *[pltpu.VMEM((NQ, 2, 2, 2, 2, RD, 128 * (hi - lo)), BF16) for lo, hi in E_TILES],
            pltpu.VMEM((8, 64, W), BF16),
            pltpu.VMEM((NQ, 6, R, W), BF16),
            pltpu.VMEM((NQ, 2, R // 2, W), BF16),
            dma((6,)),
            dma((2,)), dma((2,)),
            dma((2, 4)), dma((2, 4)),
            dma((2, 4, 4)), dma((2, 4, 4)),
            dma((NQ,)), dma((NQ,)),
            dma((NQ, 8)), dma((NQ, 8)),
            dma((NQ, 8)), dma((NQ, 8)),
            dma((NQ, 4, 4)), dma((NQ, 4, 4)),
            dma((NQ, 4, 4)), dma((NQ, 4, 4)),
            dma((NQ, 8)), dma((NQ, 8)),
        ],
        compiler_params=pltpu.CompilerParams(
            collective_id=0, has_side_effects=True, vmem_limit_bytes=56 << 20
        ),
        name="layer",
    )(head_out, residual, class_ids.reshape(1, TOKENS), head_mask, out_weight, norm_gain,
      gate_up, down_weight)


def solution(mesh):
    in_specs = (
        P("dp", "tensor"),
        P("tensor", "dp"),
        P(),
        P("tensor"),
        P("tensor", "dp"),
        P("dp"),
        P("dp", None, "tensor"),
        P("tensor", "dp"),
    )
    return jax.shard_map(local, mesh=mesh, in_specs=in_specs, out_specs=P("tensor", "dp"), check_vma=False)
```

time: 116 us -> 98.5 us (0.85)
  Pallas kernels: 108 us -> 96 us
  local copies, waits for them, and re-layouts: 5.76 us -> 1.47 us
    pallas_call x1, Pallas kernels: 108 us -> 96 us  [local(): pl.pallas_call(kernel, out_shape=jax.ShapeDtypeStruct((64, W), BF16), in_...]
    unnamed x2 -> x1, local copies, waits for them, and re-layouts: 4.5 us -> 1.47 us
    reshape x1 -> x0, local copies, waits for them, and re-layouts: 1.26 us -> none  [local(): norm_gain.reshape(1, W)]
where the time goes in v2:
time: 98.5 us; the launch traced here: 97.5 us
  Pallas kernels  96 us (97%)
  local copies, waits for them, and re-layouts  1.47 us (1%)
    pallas_call x1, Pallas kernels, local(): pl.pallas_call(kernel, out_shape=jax.ShapeDtypeStruct((64, W), BF16), in_...  96 us

profile of v2, /device:TPU:32, one launch (start us, length us, event | category | flops | bytes accessed | tf_op | source)
XLA Modules:
  0.0 97.5 jit_solution(14218417737462288259)
XLA Ops:
  0.0 96.0 %layer.1 = bf16[64,512]{1,0:T(8,128)(2,1)} custom-call(bf16[64,512]{1,0:T(8,128)(2,1)} %ho.1, bf16[64,512]{1,0:T(8,128)(2,1)} %res.1, s32[1,1024]{1,0:T(1,128)} %bitcast.1, s32[4]{0:T(128)} %mask.1, bf16[512,512]{1,0:T(8,128)(2,1)} %ow.1, bf16[512]{0:T(512)(128)(2,1)} %gain.1, bf16[512,2,896]{2,1,0:T(2,128)(2,1)} %gu.1, bf16[896,512]{1,0:T(8,128)(2,1)} %dw.1), custom_call_target="tpu_custom_call" | custom-call | tf_op jit(solution)/shard_map/layer/pallas_call | solution.py:333
  96.0 1.5 %copy.10 = bf16[64,512]{1,0:T(8,128)(2,1)} copy(bf16[64,512]{1,0:T(8,128)(2,1)} %layer.1) | data formatting | bytes 131072

commit v3 on v2

--- a/solution.py
+++ b/solution.py
@@ -29,13 +29,13 @@
 
 
 def kernel(ho, res, ids, mask, ow, gain, gu, dw, out,
-           ow_v, gu_in, gu_v, dw_v, res_v, g, oh, oht, a, ar, az, azh, ah, st, p, r1, r2, r3, r4, h0, h1, h2, h3, f, fz, fzh,
+           ow_v, gu_in, gu_v, dw_v, res_v, g, oh, oht, mean, a, ar, af, az, azh, ah, st, p, r1, r2, r3, h0, h1, h2, h3, f, fz, fzh,
            load_sem, w_s, w_r, x_s, x_r, a_s, a_r, b_s, b_r, bz_s, bz_r, cz_s, cz_r, d_s, d_r, e_s, e_r, fz_s, fz_r):
     dp = lax.axis_index("dp")
     tn = lax.axis_index("tensor")
     y, x = dp // 4, dp % 4
     z, c = tn // 2, tn % 2
-    rs = (r1, r2, r3, r4)
+    rs = (r1, r2)
     hs = (h0, h1, h2, h3)
     bits = (y // 2, (y + y // 2) % 2, x // 2, (x + x // 2) % 2)
     near = (
@@ -71,8 +71,8 @@
                                      device_id=sibling, device_id_type=MESH).wait_recv()
 
     loads = [
-        pltpu.make_async_copy(ho.at[:, 0:256], g.at[0, y, x], load_sem.at[0]),
-        pltpu.make_async_copy(ho.at[:, 256:512], g.at[1, y, x], load_sem.at[1]),
+        pltpu.make_async_copy(ho.at[:, 0:256], g.at[0, dp // 2, dp % 2], load_sem.at[0]),
+        pltpu.make_async_copy(ho.at[:, 256:512], g.at[1, dp // 2, dp % 2], load_sem.at[1]),
         pltpu.make_async_copy(gu, gu_in, load_sem.at[2]),
         pltpu.make_async_copy(dw, dw_v.at[0], load_sem.at[3]),
         pltpu.make_async_copy(ow, ow_v, load_sem.at[4]),
@@ -86,55 +86,58 @@
     for to in peers:
         pl.semaphore_signal(barrier, inc=1, device_id=to, device_id_type=MESH)
 
-    loads[2].wait()
-    gu_v[0] = gu_in[:, 0, :]
-    gu_v[1] = gu_in[:, 1, :]
+    loads[0].wait()
+    loads[1].wait()
+    pl.semaphore_wait(barrier, len(peers))
+
+    first = ((x_peer, y_peer), (y_peer, x_peer))
+    mine = [g.at[h, dp // 2, dp % 2] for h in (0, 1)]
+    for k in (1, 3, 2):
+        for h in (0, 1):
+            send(mine[h], mine[h], x_s.at[h, k], x_r.at[h, k], first[h][0](k))
+    for k in (1, 3, 2):
+        for h in (0, 1):
+            send(mine[h], mine[h], a_s.at[h, 0, k], a_r.at[h, 0, k], first[h][1](k))
+    loads[3].wait()
+    send(dw_v.at[0], dw_v.at[1], w_s.at[1], w_r.at[1], sibling)
     same = lax.broadcasted_iota(jnp.int32, (CLASSES, TOKENS), 0) == ids[...]
     onehot = same.astype(F32)
     counts = jnp.sum(onehot, axis=1, keepdims=True)
     oh[...] = onehot.astype(BF16)
-    oht[...] = onehot.T.astype(BF16)
-    loads[0].wait()
-    loads[1].wait()
-    loads[3].wait()
-    pl.semaphore_wait(barrier, len(peers))
-
-    first = ((x_peer, y_peer), (y_peer, x_peer))
-    for k in (1, 3, 2):
-        for h in (0, 1):
-            send(g.at[h, y, x], g.at[h, y, x], x_s.at[h, k], x_r.at[h, k], first[h][0](k))
-    for k in (1, 3, 2):
-        for h in (0, 1):
-            send(g.at[h, y, x], g.at[h, y, x], a_s.at[h, 0, k], a_r.at[h, 0, k], first[h][1](k))
-    send(gu_v.at[0:2], gu_v.at[2:4], w_s.at[0], w_r.at[0], sibling)
-    send(dw_v.at[0], dw_v.at[1], w_s.at[1], w_r.at[1], sibling)
     for j in (1, 3, 2):
         for h in (0, 1):
-            got = g.at[h, y, (x - j + 4) % 4] if h == 0 else g.at[h, (y - j + 4) % 4, x]
+            source = y * 4 + (x - j + 4) % 4 if h == 0 else (y - j + 4) % 4 * 4 + x
+            got = g.at[h, source // 2, source % 2]
             arrived(got, x_s.at[h, j], x_r.at[h, j])
             for k in (1, 3, 2):
                 send(got, got, a_s.at[h, j, k], a_r.at[h, j, k], first[h][1](k))
+    oht[...] = onehot.T.astype(BF16).reshape(8, 2, 64, CLASSES)
+    loads[2].wait()
+    gu_v[0] = gu_in[:, 0, :]
+    gu_v[1] = gu_in[:, 1, :]
+    send(gu_v.at[0:2], gu_v.at[2:4], w_s.at[0], w_r.at[0], sibling)
     for j in range(4):
         for k in (1, 2, 3):
             for h in (0, 1):
-                arrived(g.at[h, y, x], a_s.at[h, j, k], a_r.at[h, j, k])
-
-    means = []
+                arrived(mine[h], a_s.at[h, j, k], a_r.at[h, j, k])
+
     for h in (0, 1):
         totals = dot(oh[...], g[h].reshape(TOKENS, 256))
-        means.append((totals / jnp.maximum(counts, 1.0)).astype(BF16))
+        mean[h] = (totals / jnp.maximum(counts, 1.0)).astype(BF16)
     lane_head = lax.broadcasted_iota(jnp.int32, (1, 256), 1) // HEAD_DIM
     ablate = [jnp.where(lane_head == 0, mask[2 * h], mask[2 * h + 1]) == 1 for h in (0, 1)]
     loads[4].wait()
-    for i in range(4):
-        rows = oht[256 * i:256 * i + 256]
+
+    def share(q, core):
+        rows = oht[:, core, rows_of(q)].reshape(8 * R, CLASSES)
         total = None
         for h in (0, 1):
-            looked = dot(rows, means[h])
-            patched = jnp.where(ablate[h], looked, g[h, i].reshape(256, 256).astype(F32)).astype(BF16)
+            looked = dot(rows, mean[h])
+            kept = g[h, :, core, rows_of(q)].reshape(8 * R, 256).astype(F32)
+            patched = jnp.where(ablate[h], looked, kept).astype(BF16)
             part = dot(patched, ow_v[256 * h:256 * h + 256])
             total = part if total is None else total + part
-        a[2 * i:2 * i + 2] = total.astype(BF16).reshape(2, 2, 64, W)
+        return total.reshape(8, R, W)
 
     def rows_of(q):
         return pl.ds(R * q, R)
@@ -169,11 +172,14 @@
         return total
 
     def b1(q):
-        send(a.at[:, 1 - c, rows_of(q)], ar.at[q], b_s.at[q], b_r.at[q], sibling)
+        a[q] = share(q, 1 - c).astype(BF16)
+        send(a.at[q], ar.at[q], b_s.at[q], b_r.at[q], sibling)
 
     def b2(q):
+        both = share(q, c)
         arrived(ar.at[q], b_s.at[q], b_r.at[q])
-        both = a[:, c, rows_of(q)].astype(F32) + ar[q].astype(F32)
+        both = both + ar[q].astype(F32)
+        af[q] = both
         ah[:, rows_of(q)] = both.astype(BF16)
         z_first(q, ah, az, azh, bz_s, bz_r)
 
@@ -184,8 +190,7 @@
         if q == 0:
             loads[5].wait()
         r = rows_of(q)
-        own = a[z, c, r].astype(F32) + ar[q, z].astype(F32)
-        stream = res_v[r].astype(F32) + z_total(q, own, az, bz_s, bz_r)
+        stream = res_v[r].astype(F32) + z_total(q, af[q, z], az, bz_s, bz_r)
         st[z, r] = stream.astype(BF16)
         mine = st.at[z, r]
         for n, way in ((2, 2), (3, -2), (0, 1), (1, -1)):
@@ -250,32 +255,34 @@
             d_arrived(q, i, step - 1)
             d_send(q, i, step)
 
-    def e_ref(q, i, step):
-        order = ORDERS[i]
-        at = [slice(None)] * 4
-        for n in range(4 - step):
-            at[order[n]] = bits[order[n]]
-        return tuple(at)
-
-    def e_send(q, i, step):
-        where = (q,) + e_ref(q, i, step)
-        dim = ORDERS[i][3 - step]
-        send(hs[i].at[where], hs[i].at[where], e_s.at[q, i, step], e_r.at[q, i, step], near[dim])
-
-    def e_arrived(q, i, step):
-        at = list(e_ref(q, i, step))
-        dim = ORDERS[i][3 - step]
-        at[dim] = 1 - bits[dim]
-        arrived(hs[i].at[(q,) + tuple(at)], e_s.at[q, i, step], e_r.at[q, i, step])
-
-    def d5(q):
+    def last_axis(i):
+        return (x_peer, x, (2, 3)) if ORDERS[i][0] < 2 else (y_peer, y, (0, 1))
+
+    def bits_at(i, k):
+        _, at, dims = last_axis(i)
+        there = (at + k) % 4
+        full = list(bits)
+        full[dims[0]], full[dims[1]] = there // 2, (there + there // 2) % 2
+        return tuple(full)
+
+    def d3(q):
+        for i in range(4):
+            d_arrived(q, i, 1)
+            for k in (2, 1, 3):
+                where = (q, i) + bits_at(i, k) + d_lanes(q, i)
+                total = p[where].astype(F32) + r1[where].astype(F32) + r2[where].astype(F32)
+                p[where] = total.astype(BF16)
+                send(p.at[where], r3.at[(q, i, k) + d_lanes(q, i)], d_s.at[q, i, 1 + k], d_r.at[q, i, 1 + k], last_axis(i)[0](k))
+
+    def d4(q):
         sums = []
         for i in range(4):
-            d_arrived(q, i, 3)
             at = (q, i) + tuple(bits) + d_lanes(q, i)
-            total = p[at].astype(F32)
-            for n in range(4):
-                total = total + rs[n][at].astype(F32)
+            total = p[at].astype(F32) + r1[at].astype(F32) + r2[at].astype(F32)
+            for k in (1, 3, 2):
+                at = (q, i, k) + d_lanes(q, i)
+                arrived(r3.at[at], d_s.at[q, i, 1 + k], d_r.at[q, i, 1 + k])
+                total = total + r3[at].astype(F32)
             sums.append(total)
         inverse = lax.rsqrt(sums[q][:, FF:FF + 128] / D + EPS)
         for i in range(4):
@@ -286,12 +293,38 @@
                 hidden = gate / (1.0 + jnp.exp(-gate)) * up
                 at = 128 * (n - E_TILES[i][0])
                 hs[i][(q,) + tuple(bits) + (slice(None), slice(at, at + 128))] = hidden.astype(BF16)
+            ref = hs[i].at[(q,) + tuple(bits)]
+            for k in (2, 1, 3):
+                send(ref, ref, e_s.at[q, i, k - 1], e_r.at[q, i, k - 1], last_axis(i)[0](k))
+
+    def e_ref(q, i, step):
+        order = ORDERS[i]
+        at = [slice(None)] * 4
+        for n in range(2 - step):
+            at[order[n]] = bits[order[n]]
+        return at
+
+    def e_send(q, i, step):
+        where = (q,) + tuple(e_ref(q, i, step))
+        send(hs[i].at[where], hs[i].at[where], e_s.at[q, i, 3 + step], e_r.at[q, i, 3 + step], near[ORDERS[i][1 - step]])
+
+    def e_arrived(q, i, step):
+        at = e_ref(q, i, step)
+        dim = ORDERS[i][1 - step]
+        at[dim] = 1 - bits[dim]
+        arrived(hs[i].at[(q,) + tuple(at)], e_s.at[q, i, 3 + step], e_r.at[q, i, 3 + step])
+
+    def e2(q):
+        for i in range(4):
+            ref = hs[i].at[(q,) + tuple(bits)]
+            for k in (1, 3, 2):
+                arrived(ref, e_s.at[q, i, k - 1], e_r.at[q, i, k - 1])
             e_send(q, i, 0)
 
-    def e_next(q, step):
-        for i in range(4):
-            e_arrived(q, i, step - 1)
-            e_send(q, i, step)
+    def e3(q):
+        for i in range(4):
+            e_arrived(q, i, 0)
+            e_send(q, i, 1)
 
     def f1(q):
         if q == 0:
@@ -299,7 +332,7 @@
         down = dw_v[...].reshape(2 * FF, W)
         total = None
         for i in range(4):
-            e_arrived(q, i, 3)
+            e_arrived(q, i, 1)
             lo, hi = E_TILES[i]
             part = dot(hs[i][q].reshape(8 * R, 128 * (hi - lo)), down[128 * lo:128 * hi])
             total = part if total is None else total + part
@@ -314,10 +347,8 @@
         total = z_total(q, f[z, r].astype(F32), fz, fz_s, fz_r)
         out[r] = (st[z, r].astype(F32) + total).astype(BF16)
 
-    stages = [b1, b2, b3, c1, c2, d1]
-    stages += [functools.partial(d_next, step=s) for s in (1, 2, 3)] + [d5]
-    stages += [functools.partial(e_next, step=s) for s in (1, 2, 3)] + [f1, f2, f3]
-    for stage in stages:
+    d2 = functools.partial(d_next, step=1)
+    for stage in (b1, b2, b3, c1, c2, d1, d2, d3, d4, e2, e3, f1, f2, f3):
         for q in range(NQ):
             stage(q)
     for cp in sends:
@@ -341,16 +372,19 @@
             pltpu.VMEM((4, W, FF), BF16),
             pltpu.VMEM((2, FF, W), BF16),
             pltpu.VMEM((64, W), BF16),
-            pltpu.VMEM((2, 4, 4, 64, 256), BF16),
+            pltpu.VMEM((2, 8, 2, 64, 256), BF16),
             pltpu.VMEM((CLASSES, TOKENS), BF16),
-            pltpu.VMEM((TOKENS, CLASSES), BF16),
-            pltpu.VMEM((8, 2, 64, W), BF16),
+            pltpu.VMEM((8, 2, 64, CLASSES), BF16),
+            pltpu.VMEM((2, CLASSES, 256), BF16),
             pltpu.VMEM((NQ, 8, R, W), BF16),
+            pltpu.VMEM((NQ, 8, R, W), BF16),
+            pltpu.VMEM((NQ, 8, R, W), F32),
             pltpu.VMEM((NQ, 6, R, W), BF16),
             pltpu.VMEM((NQ, 2, R // 2, W), BF16),
             pltpu.VMEM((8, 64, W), BF16),
             pltpu.VMEM((8, 64, W), BF16),
-            *[pltpu.VMEM(cube, BF16) for _ in range(5)],
+            *[pltpu.VMEM(cube, BF16) for _ in range(3)],
+            pltpu.VMEM((NQ, 4, 4, RD, FF + 128), BF16),
             *[pltpu.VMEM((NQ, 2, 2, 2, 2, RD, 128 * (hi - lo)), BF16) for lo, hi in E_TILES],
             pltpu.VMEM((8, 64, W), BF16),
             pltpu.VMEM((NQ, 6, R, W), BF16),
@@ -362,8 +396,8 @@
             dma((NQ,)), dma((NQ,)),
             dma((NQ, 8)), dma((NQ, 8)),
             dma((NQ, 8)), dma((NQ, 8)),
-            dma((NQ, 4, 4)), dma((NQ, 4, 4)),
-            dma((NQ, 4, 4)), dma((NQ, 4, 4)),
+            dma((NQ, 4, 5)), dma((NQ, 4, 5)),
+            dma((NQ, 4, 5)), dma((NQ, 4, 5)),
             dma((NQ, 8)), dma((NQ, 8)),
         ],
         compiler_params=pltpu.CompilerParams(

time: 98.5 us -> 91.6 us (0.930)
  Pallas kernels: 96 us -> 89.9 us
    pallas_call x1, Pallas kernels: 96 us -> 89.9 us  [local(): pl.pallas_call(kernel, out_shape=jax.ShapeDtypeStruct((64, W), BF16), in_...]
where the time goes in v3:
time: 91.6 us; the launch traced here: 91.4 us
  Pallas kernels  89.9 us (98%)
  local copies, waits for them, and re-layouts  1.47 us (2%)
    pallas_call x1, Pallas kernels, local(): pl.pallas_call(kernel, out_shape=jax.ShapeDtypeStruct((64, W), BF16), in_...  89.9 us

profile of v3, /device:TPU:32, one launch (start us, length us, event | category | flops | bytes accessed | tf_op | source)
XLA Modules:
  0.0 91.4 jit_solution(5992162881820467111)
XLA Ops:
  0.0 89.9 %layer.1 = bf16[64,512]{1,0:T(8,128)(2,1)} custom-call(bf16[64,512]{1,0:T(8,128)(2,1)} %ho.1, bf16[64,512]{1,0:T(8,128)(2,1)} %res.1, s32[1,1024]{1,0:T(1,128)} %bitcast.1, s32[4]{0:T(128)} %mask.1, bf16[512,512]{1,0:T(8,128)(2,1)} %ow.1, bf16[512]{0:T(512)(128)(2,1)} %gain.1, bf16[512,2,896]{2,1,0:T(2,128)(2,1)} %gu.1, bf16[896,512]{1,0:T(8,128)(2,1)} %dw.1), custom_call_target="tpu_custom_call" | custom-call | tf_op jit(solution)/shard_map/layer/pallas_call | solution.py:364
  90.0 1.5 %copy.10 = bf16[64,512]{1,0:T(8,128)(2,1)} copy(bf16[64,512]{1,0:T(8,128)(2,1)} %layer.1) | data formatting | bytes 131072

commit v4 on v3

--- a/solution.py
+++ b/solution.py
@@ -1,5 +1,3 @@
-import functools
-
 import jax
 import jax.numpy as jnp
 from jax import lax
@@ -21,7 +19,8 @@
 R = 64 // NQ
 RD = R // 2
 ORDERS = ((3, 2, 1, 0), (2, 3, 0, 1), (1, 0, 3, 2), (0, 1, 2, 3))
-E_TILES = ((0, 4), (4, 8), (8, 11), (11, 14))
+D_TILES = (((0, 4), (4, 8), (8, 11), (11, 14)), ((0, 3), (3, 6), (6, 10), (10, 14)))
+E_TILES = (((0, 2), (2, 4), (4, 6), (6, 7)), ((0, 1), (1, 3), (3, 5), (5, 7)))
 
 
 def dot(a, b):
@@ -29,8 +28,8 @@
 
 
 def kernel(ho, res, ids, mask, ow, gain, gu, dw, out,
-           ow_v, gu_in, gu_v, dw_v, res_v, g, oh, oht, mean, a, ar, af, az, azh, ah, st, p, r1, r2, r3, h0, h1, h2, h3, f, fz, fzh,
-           load_sem, w_s, w_r, x_s, x_r, a_s, a_r, b_s, b_r, bz_s, bz_r, cz_s, cz_r, d_s, d_r, e_s, e_r, fz_s, fz_r):
+           ow_v, gu_in, gu_v, dw_v, res_v, g, oh, oht, mean, a, ar, af, az, azh, ah, st, sc, inv, sq, sqx, sqy, p, r1, r2, r3, h0, h1, h2, h3, f, fz, fzh,
+           load_sem, w_s, w_r, x_s, x_r, a_s, a_r, b_s, b_r, bz_s, bz_r, cz_s, cz_r, d_s, d_r, q_s, q_r, e_s, e_r, fz_s, fz_r):
     dp = lax.axis_index("dp")
     tn = lax.axis_index("tensor")
     y, x = dp // 4, dp % 4
@@ -67,6 +66,8 @@
         sends.append(cp)
 
     def arrived(ref, ssem, rsem):
+        while len(sends) > 48:
+            sends.pop(0).wait_send()
         pltpu.make_async_remote_copy(src_ref=ref, dst_ref=ref, send_sem=ssem, recv_sem=rsem,
                                      device_id=sibling, device_id_type=MESH).wait_recv()
 
@@ -86,18 +87,17 @@
     for to in peers:
         pl.semaphore_signal(barrier, inc=1, device_id=to, device_id_type=MESH)
 
-    loads[0].wait()
-    loads[1].wait()
     pl.semaphore_wait(barrier, len(peers))
 
     first = ((x_peer, y_peer), (y_peer, x_peer))
-    mine = [g.at[h, dp // 2, dp % 2] for h in (0, 1)]
+    mine = [ho.at[:, 256 * h:256 * h + 256] for h in (0, 1)]
+    slot = [g.at[h, dp // 2, dp % 2] for h in (0, 1)]
     for k in (1, 3, 2):
         for h in (0, 1):
-            send(mine[h], mine[h], x_s.at[h, k], x_r.at[h, k], first[h][0](k))
+            send(mine[h], slot[h], x_s.at[h, k], x_r.at[h, k], first[h][0](k))
     for k in (1, 3, 2):
         for h in (0, 1):
-            send(mine[h], mine[h], a_s.at[h, 0, k], a_r.at[h, 0, k], first[h][1](k))
+            send(mine[h], slot[h], a_s.at[h, 0, k], a_r.at[h, 0, k], first[h][1](k))
     loads[3].wait()
     send(dw_v.at[0], dw_v.at[1], w_s.at[1], w_r.at[1], sibling)
     same = lax.broadcasted_iota(jnp.int32, (CLASSES, TOKENS), 0) == ids[...]
@@ -112,14 +112,13 @@
             for k in (1, 3, 2):
                 send(got, got, a_s.at[h, j, k], a_r.at[h, j, k], first[h][1](k))
     oht[...] = onehot.T.astype(BF16).reshape(8, 2, 64, CLASSES)
-    loads[2].wait()
-    gu_v[0] = gu_in[:, 0, :]
-    gu_v[1] = gu_in[:, 1, :]
-    send(gu_v.at[0:2], gu_v.at[2:4], w_s.at[0], w_r.at[0], sibling)
     for j in range(4):
         for k in (1, 2, 3):
             for h in (0, 1):
-                arrived(mine[h], a_s.at[h, j, k], a_r.at[h, j, k])
+                arrived(slot[h], a_s.at[h, j, k], a_r.at[h, j, k])
+
+    loads[0].wait()
+    loads[1].wait()
 
     for h in (0, 1):
         totals = dot(oh[...], g[h].reshape(TOKENS, 256))
@@ -213,47 +212,71 @@
         at[order[step]] = 1 - bits[order[step]] if flip else bits[order[step]]
         return tuple(at)
 
-    def d_lanes(q, i):
-        return (slice(None), pl.ds(0, FF + 128 if i == q else FF))
-
-    def d_send(q, i, step):
+    def at_chunk(u, i):
+        return (2 * u[0] + u[1], i)
+
+    def d_lanes(u, i):
+        lo, hi = D_TILES[u[1]][i]
+        return (slice(None), pl.ds(0, 128 * (hi - lo)))
+
+    def d_send(u, i, step):
         order = ORDERS[i]
-        where = (q, i) + cube(order, step, True) + d_lanes(q, i)
+        where = at_chunk(u, i) + cube(order, step, True) + d_lanes(u, i)
         if step > 0:
-            total = p[where].astype(F32)
-            for n in range(step):
-                total = total + rs[n][where].astype(F32)
+            total = p[where].astype(F32) + r1[where].astype(F32)
             p[where] = total.astype(BF16)
-        send(p.at[where], rs[step].at[where], d_s.at[q, i, step], d_r.at[q, i, step], near[order[step]])
-
-    def d_arrived(q, i, step):
-        where = (q, i) + cube(ORDERS[i], step, False) + d_lanes(q, i)
-        arrived(rs[step].at[where], d_s.at[q, i, step], d_r.at[q, i, step])
-
-    def d1(q):
-        if q == 0:
-            arrived(gu_v.at[0:2], w_s.at[0], w_r.at[0])
-        r = rows_of(q)
-        mine = st.at[z, r]
-        for n in (0, 1, 4, 5):
-            arrived(mine, cz_s.at[q, n], cz_r.at[q, n])
-        for n in (6, 7):
-            arrived(st.at[z, pl.ds(R * q, R // 2)], cz_s.at[q, n], cz_r.at[q, n])
-        wide = st[:, r].reshape(8 * R, W).astype(F32)
-        scaled = (wide * gain[...].astype(F32).reshape(1, W)).astype(BF16)
-        for i in range(4):
-            part = dot(scaled, gu_v[i]).astype(BF16)
-            p[q, i, :, :, :, :, :, 0:FF] = part.reshape(2, 2, 2, 2, RD, FF)
-            if i == q:
-                squares = jnp.sum(wide * wide, axis=1, keepdims=True)
-                squares = jnp.broadcast_to(squares, (8 * R, 128)).astype(BF16)
-                p[q, i, :, :, :, :, :, FF:FF + 128] = squares.reshape(2, 2, 2, 2, RD, 128)
-            d_send(q, i, 0)
-
-    def d_next(q, step):
-        for i in range(4):
-            d_arrived(q, i, step - 1)
-            d_send(q, i, step)
+        sem = at_chunk(u, i) + (step,)
+        send(p.at[where], rs[step].at[where], d_s.at[sem], d_r.at[sem], near[order[step]])
+
+    def d_arrived(u, i, step):
+        where = at_chunk(u, i) + cube(ORDERS[i], step, False) + d_lanes(u, i)
+        sem = at_chunk(u, i) + (step,)
+        arrived(rs[step].at[where], d_s.at[sem], d_r.at[sem])
+
+    def d1(u):
+        q, units = u
+        if u == (0, 1):
+            arrived(gu_v.at[0], w_s.at[0], w_r.at[0])
+        if units == 0:
+            r = rows_of(q)
+            mine = st.at[z, r]
+            for n in (0, 1, 4, 5):
+                arrived(mine, cz_s.at[q, n], cz_r.at[q, n])
+            for n in (6, 7):
+                arrived(st.at[z, pl.ds(R * q, R // 2)], cz_s.at[q, n], cz_r.at[q, n])
+            wide = st[:, r].reshape(8 * R, W).astype(F32)
+            scaled = (wide * gain[...].astype(F32).reshape(1, W)).astype(BF16)
+            sc[q] = scaled.reshape(2, 2, 2, 2, RD, W)
+            squares = jnp.sum(wide * wide, axis=1, keepdims=True)
+            lane = lax.broadcasted_iota(jnp.int32, (8 * R, 128), 1)
+            row = lax.broadcasted_iota(jnp.int32, (8 * R, 128), 0) % RD
+            sq[q, 0] = jnp.where(lane == row, squares, 0.0).reshape(16, RD, 128).sum(axis=1)
+            for k in (1, 3, 2):
+                send(sq.at[q, 0], sqx.at[q, k], q_s.at[q, 0, k], q_r.at[q, 0, k], x_peer(k))
+
+        for sent in (True, False):
+            for i in range(4):
+                lo, hi = D_TILES[units][i]
+                width = 128 * (hi - lo)
+                half = cube(ORDERS[i], 0, sent)
+                part = dot(sc[(q,) + half].reshape(8 * RD, W), gu_v[units, :, 128 * lo:128 * hi]).astype(BF16)
+                p[at_chunk(u, i) + half + (slice(None), slice(0, width))] = part.reshape(2, 2, 2, RD, width)
+                if sent:
+                    d_send(u, i, 0)
+
+    def d2(u):
+        q, units = u
+        if units == 0:
+            total = sq[q, 0]
+            for k in (1, 3, 2):
+                arrived(sqx.at[q, k], q_s.at[q, 0, k], q_r.at[q, 0, k])
+                total = total + sqx[q, k]
+            sq[q, 1] = total
+            for k in (1, 3, 2):
+                send(sq.at[q, 1], sqy.at[q, k], q_s.at[q, 1, k], q_r.at[q, 1, k], y_peer(k))
+        for i in range(4):
+            d_arrived(u, i, 0)
+            d_send(u, i, 1)
 
     def last_axis(i):
         return (x_peer, x, (2, 3)) if ORDERS[i][0] < 2 else (y_peer, y, (0, 1))
@@ -265,77 +288,100 @@
         full[dims[0]], full[dims[1]] = there // 2, (there + there // 2) % 2
         return tuple(full)
 
-    def d3(q):
-        for i in range(4):
-            d_arrived(q, i, 1)
+    def d3(u):
+        for i in range(4):
+            d_arrived(u, i, 1)
             for k in (2, 1, 3):
-                where = (q, i) + bits_at(i, k) + d_lanes(q, i)
+                where = at_chunk(u, i) + bits_at(i, k) + d_lanes(u, i)
                 total = p[where].astype(F32) + r1[where].astype(F32) + r2[where].astype(F32)
                 p[where] = total.astype(BF16)
-                send(p.at[where], r3.at[(q, i, k) + d_lanes(q, i)], d_s.at[q, i, 1 + k], d_r.at[q, i, 1 + k], last_axis(i)[0](k))
-
-    def d4(q):
-        sums = []
-        for i in range(4):
-            at = (q, i) + tuple(bits) + d_lanes(q, i)
+                sem = at_chunk(u, i) + (1 + k,)
+                send(p.at[where], r3.at[at_chunk(u, i) + (k,) + d_lanes(u, i)], d_s.at[sem], d_r.at[sem], last_axis(i)[0](k))
+
+    def h_ref(u, i, at):
+        lo, hi = E_TILES[u[1]][i]
+        return hs[i].at[(2 * u[0] + u[1],) + tuple(at) + (slice(None), pl.ds(0, 128 * (hi - lo)))]
+
+    def d4(u):
+        q, units = u
+        if units == 0:
+            squares = sq[q, 1]
+            for k in (1, 3, 2):
+                arrived(sqy.at[q, k], q_s.at[q, 1, k], q_r.at[q, 1, k])
+                squares = squares + sqy[q, k]
+            here = 8 * bits[0] + 4 * bits[1] + 2 * bits[2] + bits[3]
+            row = lax.broadcasted_iota(jnp.int32, (16, 128), 0)
+            squares = jnp.sum(jnp.where(row == here, squares, 0.0), axis=0, keepdims=True)
+            row = lax.broadcasted_iota(jnp.int32, (RD, 128), 0)
+            lane = lax.broadcasted_iota(jnp.int32, (RD, 128), 1)
+            squares = jnp.sum(jnp.where(row == lane, squares, 0.0), axis=1, keepdims=True)
+            inv[q] = jnp.broadcast_to(lax.rsqrt(squares / D + EPS), (RD, 128))
+        tiles = []
+        for i in range(4):
+            at = at_chunk(u, i) + tuple(bits) + d_lanes(u, i)
             total = p[at].astype(F32) + r1[at].astype(F32) + r2[at].astype(F32)
             for k in (1, 3, 2):
-                at = (q, i, k) + d_lanes(q, i)
-                arrived(r3.at[at], d_s.at[q, i, 1 + k], d_r.at[q, i, 1 + k])
+                at = at_chunk(u, i) + (k,) + d_lanes(u, i)
+                sem = at_chunk(u, i) + (1 + k,)
+                arrived(r3.at[at], d_s.at[sem], d_r.at[sem])
                 total = total + r3[at].astype(F32)
-            sums.append(total)
-        inverse = lax.rsqrt(sums[q][:, FF:FF + 128] / D + EPS)
-        for i in range(4):
-            for n in range(*E_TILES[i]):
-                lanes = slice(128 * (n % 7), 128 * (n % 7) + 128)
-                gate = sums[2 * (n // 7)][:, lanes] * inverse
-                up = sums[2 * (n // 7) + 1][:, lanes] * inverse
+            lo, hi = D_TILES[units][i]
+            tiles += [total[:, 128 * n:128 * n + 128] for n in range(hi - lo)]
+        inverse = inv[q]
+        for i in range(4):
+            lo, hi = E_TILES[units][i]
+            for n in range(lo, hi):
+                gate, up = tiles[n] * inverse, tiles[7 + n] * inverse
                 hidden = gate / (1.0 + jnp.exp(-gate)) * up
-                at = 128 * (n - E_TILES[i][0])
-                hs[i][(q,) + tuple(bits) + (slice(None), slice(at, at + 128))] = hidden.astype(BF16)
-            ref = hs[i].at[(q,) + tuple(bits)]
+                hs[i][(2 * q + units,) + tuple(bits) + (slice(None), slice(128 * (n - lo), 128 * (n - lo) + 128))] = hidden.astype(BF16)
+            ref = h_ref(u, i, bits)
             for k in (2, 1, 3):
-                send(ref, ref, e_s.at[q, i, k - 1], e_r.at[q, i, k - 1], last_axis(i)[0](k))
-
-    def e_ref(q, i, step):
+                sem = at_chunk(u, i) + (k - 1,)
+                send(ref, ref, e_s.at[sem], e_r.at[sem], last_axis(i)[0](k))
+
+    def e_at(i, step):
         order = ORDERS[i]
         at = [slice(None)] * 4
         for n in range(2 - step):
             at[order[n]] = bits[order[n]]
         return at
 
-    def e_send(q, i, step):
-        where = (q,) + tuple(e_ref(q, i, step))
-        send(hs[i].at[where], hs[i].at[where], e_s.at[q, i, 3 + step], e_r.at[q, i, 3 + step], near[ORDERS[i][1 - step]])
-
-    def e_arrived(q, i, step):
-        at = e_ref(q, i, step)
+    def e_send(u, i, step):
+        ref = h_ref(u, i, e_at(i, step))
+        sem = at_chunk(u, i) + (3 + step,)
+        send(ref, ref, e_s.at[sem], e_r.at[sem], near[ORDERS[i][1 - step]])
+
+    def e_arrived(u, i, step):
+        at = e_at(i, step)
         dim = ORDERS[i][1 - step]
         at[dim] = 1 - bits[dim]
-        arrived(hs[i].at[(q,) + tuple(at)], e_s.at[q, i, 3 + step], e_r.at[q, i, 3 + step])
-
-    def e2(q):
-        for i in range(4):
-            ref = hs[i].at[(q,) + tuple(bits)]
-            for k in (1, 3, 2):
-                arrived(ref, e_s.at[q, i, k - 1], e_r.at[q, i, k - 1])
-            e_send(q, i, 0)
-
-    def e3(q):
-        for i in range(4):
-            e_arrived(q, i, 0)
-            e_send(q, i, 1)
+        sem = at_chunk(u, i) + (3 + step,)
+        arrived(h_ref(u, i, at), e_s.at[sem], e_r.at[sem])
+
+    def e2(u):
+        for i in range(4):
+            ref = h_ref(u, i, bits)
+            for k in (1, 3, 2):
+                sem = at_chunk(u, i) + (k - 1,)
+                arrived(ref, e_s.at[sem], e_r.at[sem])
+            e_send(u, i, 0)
+
+    def e3(u):
+        for i in range(4):
+            e_arrived(u, i, 0)
+            e_send(u, i, 1)
 
     def f1(q):
         if q == 0:
             arrived(dw_v.at[1], w_s.at[1], w_r.at[1])
-        down = dw_v[...].reshape(2 * FF, W)
         total = None
-        for i in range(4):
-            e_arrived(q, i, 1)
-            lo, hi = E_TILES[i]
-            part = dot(hs[i][q].reshape(8 * R, 128 * (hi - lo)), down[128 * lo:128 * hi])
-            total = part if total is None else total + part
+        for units in (0, 1):
+            for i in range(4):
+                e_arrived((q, units), i, 1)
+                lo, hi = E_TILES[units][i]
+                rows = hs[i][2 * q + units, :, :, :, :, :, 0:128 * (hi - lo)].reshape(8 * R, 128 * (hi - lo))
+                part = dot(rows, dw_v[units, 128 * lo:128 * hi])
+                total = part if total is None else total + part
         f[:, rows_of(q)] = total.astype(BF16).reshape(8, R, W)
         z_first(q, f, fz, fzh, fz_s, fz_r)
 
@@ -347,9 +393,25 @@
         total = z_total(q, f[z, r].astype(F32), fz, fz_s, fz_r)
         out[r] = (st[z, r].astype(F32) + total).astype(BF16)
 
-    d2 = functools.partial(d_next, step=1)
-    for stage in (b1, b2, b3, c1, c2, d1, d2, d3, d4, e2, e3, f1, f2, f3):
-        for q in range(NQ):
+    parts = list(range(NQ))
+    chunks = [(q, units) for q in parts for units in (0, 1)]
+    for stage in (b1, b2):
+        for q in parts:
+            stage(q)
+    loads[2].wait()
+    gu_v[0, :, 0:FF] = gu_in[:, 0, :]
+    for q in parts:
+        b3(q)
+    gu_v[0, :, FF:2 * FF] = gu_in[:, 1, :]
+    send(gu_v.at[0], gu_v.at[1], w_s.at[0], w_r.at[0], sibling)
+    for stage in (c1, c2):
+        for q in parts:
+            stage(q)
+    for stage in (d1, d2, d3, d4, e2, e3):
+        for u in chunks:
+            stage(u)
+    for stage in (f1, f2, f3):
+        for q in parts:
             stage(q)
     for cp in sends:
         cp.wait_send()
@@ -360,7 +422,7 @@
     vmem = pl.BlockSpec(memory_space=pltpu.VMEM)
     smem = pl.BlockSpec(memory_space=pltpu.SMEM)
     dma = pltpu.SemaphoreType.DMA
-    cube = (NQ, 4, 2, 2, 2, 2, RD, FF + 128)
+    cube = (2 * NQ, 4, 2, 2, 2, 2, RD, 512)
     return pl.pallas_call(
         kernel,
         out_shape=jax.ShapeDtypeStruct((64, W), BF16),
@@ -369,7 +431,7 @@
         scratch_shapes=[
             pltpu.VMEM((W, W), BF16),
             pltpu.VMEM((W, 2, FF), BF16),
-            pltpu.VMEM((4, W, FF), BF16),
+            pltpu.VMEM((2, W, 2 * FF), BF16),
             pltpu.VMEM((2, FF, W), BF16),
             pltpu.VMEM((64, W), BF16),
             pltpu.VMEM((2, 8, 2, 64, 256), BF16),
@@ -383,9 +445,14 @@
             pltpu.VMEM((NQ, 2, R // 2, W), BF16),
             pltpu.VMEM((8, 64, W), BF16),
             pltpu.VMEM((8, 64, W), BF16),
+            pltpu.VMEM((NQ, 2, 2, 2, 2, RD, W), BF16),
+            pltpu.VMEM((NQ, RD, 128), F32),
+            pltpu.VMEM((NQ, 2, 16, 128), F32),
+            pltpu.VMEM((NQ, 4, 16, 128), F32),
+            pltpu.VMEM((NQ, 4, 16, 128), F32),
             *[pltpu.VMEM(cube, BF16) for _ in range(3)],
-            pltpu.VMEM((NQ, 4, 4, RD, FF + 128), BF16),
-            *[pltpu.VMEM((NQ, 2, 2, 2, 2, RD, 128 * (hi - lo)), BF16) for lo, hi in E_TILES],
+            pltpu.VMEM((2 * NQ, 4, 4, RD, 512), BF16),
+            *[pltpu.VMEM((2 * NQ, 2, 2, 2, 2, RD, 256), BF16) for _ in range(4)],
             pltpu.VMEM((8, 64, W), BF16),
             pltpu.VMEM((NQ, 6, R, W), BF16),
             pltpu.VMEM((NQ, 2, R // 2, W), BF16),
@@ -396,8 +463,9 @@
             dma((NQ,)), dma((NQ,)),
             dma((NQ, 8)), dma((NQ, 8)),
             dma((NQ, 8)), dma((NQ, 8)),
-            dma((NQ, 4, 5)), dma((NQ, 4, 5)),
-            dma((NQ, 4, 5)), dma((NQ, 4, 5)),
+            dma((2 * NQ, 4, 5)), dma((2 * NQ, 4, 5)),
+            dma((NQ, 2, 4)), dma((NQ, 2, 4)),
+            dma((2 * NQ, 4, 5)), dma((2 * NQ, 4, 5)),
             dma((NQ, 8)), dma((NQ, 8)),
         ],
         compiler_params=pltpu.CompilerParams(

time: 91.6 us -> 89.7 us (0.979)
  Pallas kernels: 89.9 us -> 88 us
    pallas_call x1, Pallas kernels: 89.9 us -> 88 us  [local(): pl.pallas_call(kernel, out_shape=jax.ShapeDtypeStruct((64, W), BF16), in_...]
where the time goes in v4:
time: 89.7 us; the launch traced here: 89.5 us
  Pallas kernels  88 us (98%)
  local copies, waits for them, and re-layouts  1.47 us (2%)
    pallas_call x1, Pallas kernels, local(): pl.pallas_call(kernel, out_shape=jax.ShapeDtypeStruct((64, W), BF16), in_...  88 us

profile of v4, /device:TPU:32, one launch (start us, length us, event | category | flops | bytes accessed | tf_op | source)
XLA Modules:
  0.0 89.5 jit_solution(3046744842658265140)
XLA Ops:
  0.0 88.0 %layer.1 = bf16[64,512]{1,0:T(8,128)(2,1)} custom-call(bf16[64,512]{1,0:T(8,128)(2,1)} %ho.1, bf16[64,512]{1,0:T(8,128)(2,1)} %res.1, s32[1,1024]{1,0:T(1,128)} %bitcast.1, s32[4]{0:T(128)} %mask.1, bf16[512,512]{1,0:T(8,128)(2,1)} %ow.1, bf16[512]{0:T(512)(128)(2,1)} %gain.1, bf16[512,2,896]{2,1,0:T(2,128)(2,1)} %gu.1, bf16[896,512]{1,0:T(8,128)(2,1)} %dw.1), custom_call_target="tpu_custom_call" | custom-call | tf_op jit(solution)/shard_map/layer/pallas_call | solution.py:426
  88.0 1.5 %copy.10 = bf16[64,512]{1,0:T(8,128)(2,1)} copy(bf16[64,512]{1,0:T(8,128)(2,1)} %layer.1) | data formatting | bytes 131072

commit v5 on v4

--- a/solution.py
+++ b/solution.py
@@ -291,7 +291,7 @@
     def d3(u):
         for i in range(4):
             d_arrived(u, i, 1)
-            for k in (2, 1, 3):
+            for k in (1, 3, 2):
                 where = at_chunk(u, i) + bits_at(i, k) + d_lanes(u, i)
                 total = p[where].astype(F32) + r1[where].astype(F32) + r2[where].astype(F32)
                 p[where] = total.astype(BF16)
@@ -335,7 +335,7 @@
                 hidden = gate / (1.0 + jnp.exp(-gate)) * up
                 hs[i][(2 * q + units,) + tuple(bits) + (slice(None), slice(128 * (n - lo), 128 * (n - lo) + 128))] = hidden.astype(BF16)
             ref = h_ref(u, i, bits)
-            for k in (2, 1, 3):
+            for k in (1, 3, 2):
                 sem = at_chunk(u, i) + (k - 1,)
                 send(ref, ref, e_s.at[sem], e_r.at[sem], last_axis(i)[0](k))
 

time: 89.7 us -> 89.6 us (level)
  no operation moved by 1% of the time
where the time goes in v5:
time: 89.6 us; the launch traced here: 89.4 us
  Pallas kernels  87.9 us (98%)
  local copies, waits for them, and re-layouts  1.47 us (2%)
    pallas_call x1, Pallas kernels, local(): pl.pallas_call(kernel, out_shape=jax.ShapeDtypeStruct((64, W), BF16), in_...  87.9 us

profile of v5, /device:TPU:32, one launch (start us, length us, event | category | flops | bytes accessed | tf_op | source)
XLA Modules:
  0.0 89.4 jit_solution(1264752291857950194)
XLA Ops:
  0.0 87.9 %layer.1 = bf16[64,512]{1,0:T(8,128)(2,1)} custom-call(bf16[64,512]{1,0:T(8,128)(2,1)} %ho.1, bf16[64,512]{1,0:T(8,128)(2,1)} %res.1, s32[1,1024]{1,0:T(1,128)} %bitcast.1, s32[4]{0:T(128)} %mask.1, bf16[512,512]{1,0:T(8,128)(2,1)} %ow.1, bf16[512]{0:T(512)(128)(2,1)} %gain.1, bf16[512,2,896]{2,1,0:T(2,128)(2,1)} %gu.1, bf16[896,512]{1,0:T(8,128)(2,1)} %dw.1), custom_call_target="tpu_custom_call" | custom-call | tf_op jit(solution)/shard_map/layer/pallas_call | solution.py:426
  87.9 1.5 %copy.10 = bf16[64,512]{1,0:T(8,128)(2,1)} copy(bf16[64,512]{1,0:T(8,128)(2,1)} %layer.1) | data formatting | bytes 131072
